TPU v7x, 512 devices: a whole 4x8x8 slice. The times are simulated.
512 devices in a mesh: seq: 64 (over y_lo, z, x), chan: 8 (over y_hi, core).
Axes of the slice: x: 4, y: 8 (y_hi: 4, y_lo: 2; y = y_hi * 2 + y_lo), z: 8, core: 2. Of those that a mesh axis runs over, the one named last changes fastest.
Arguments:
- gate_acts: bfloat16 [65536, 2048], P('seq', 'chan'), may hold values from -40 to 40
- value_acts: bfloat16 [65536, 2048], P('seq', 'chan'), may hold values from -6 to 6
- kernel: bfloat16 [32, 2048], P('chan'), may hold values from -0.125 to 0.125
- norm_gain: float32 [2048], P('chan'), may hold values from 0.1 to 1.9
- out_grad: bfloat16 [65536, 2048], P('seq', 'chan'), may hold values from -30 to 30
Outputs:
- normed: bfloat16 [65536, 2048], P('seq', 'chan')
- gate_grad: bfloat16 [65536, 2048], P('seq', 'chan')
- value_grad: bfloat16 [65536, 2048], P('seq', 'chan')
- kernel_grad: float32 [32, 2048], P('chan')
- gain_grad: float32 [2048], P('chan')
All inputs are finite; a program needn't handle non-finite values.
Results may differ from a plain program's by a relative error of at most 0.0085.
Values may be sent and summed in bfloat16 or wider, within the bound.
A program may use at most 128 MiB of HBM per device.

v0:
```python
import math

import jax
import jax.numpy as jnp
from jax import lax
from jax.sharding import PartitionSpec as P

D = 2048


tile_cap = 256
norm_eps = 1e-06


def from_behind(value, axis, by):
    count = lax.axis_size(axis)
    pairs = [(i, i + by) for i in range(count) if 0 <= i + by < count]
    return lax.ppermute(value, axis, pairs)


def extended_2(block, sides, width):
    for axis, dim in sides:
        count = lax.axis_size(axis)
        forward = [(i, i + 1) for i in range(count - 1)]
        backward = [(target, source) for source, target in forward]
        low = lax.ppermute(
            lax.slice_in_dim(block, block.shape[dim] - width, None, axis=dim), axis, forward
        )
        high = lax.ppermute(lax.slice_in_dim(block, 0, width, axis=dim), axis, backward)
        block = jnp.concatenate([low, block, high], axis=dim)
    return block


def banded(row_vec, tile_rows, window_len):
    head_here = row_vec.shape[0]
    row_full = window_len + tile_rows
    wide_rows = jnp.broadcast_to(row_vec[:, None, :], (head_here, tile_rows, row_full))
    flat_rows = wide_rows.reshape(head_here, tile_rows * row_full)[:, : tile_rows * (row_full - 1)]
    return flat_rows.reshape(head_here, tile_rows, row_full - 1)[:, :, :window_len]


def windows(extended, tile_rows, out_count, slot_count):
    head_here, head_width, row_total = extended.shape
    tile_grid = extended.reshape(head_here, head_width, row_total // tile_rows, tile_rows)
    return jnp.concatenate(
        [
            tile_grid[:, :, slot_index : slot_index + out_count, :]
            for slot_index in range(slot_count)
        ],
        axis=3,
    )


def diagonal_sums(cross, lag_width):
    head_here, tile_rows, window_len = cross.shape
    flat_rows = cross.reshape(head_here, tile_rows * window_len)
    cut_at = (tile_rows - 1) * (window_len + 1)
    upper = flat_rows[:, :cut_at].reshape(head_here, tile_rows - 1, window_len + 1)[
        :, :, :lag_width
    ]
    return jnp.sum(upper, axis=1) + flat_rows[:, cut_at : cut_at + lag_width]


def on_device(gate_acts, value_acts, kernel, norm_gain, out_grad):
    row_count, chan_width = value_acts.shape
    head_here = kernel.shape[0]
    head_width = chan_width // head_here
    lag_span = kernel.shape[1] // 2
    tile_rows = min(tile_cap, lag_span)
    slot_count = 1 + 2 * lag_span // tile_rows
    window_len = tile_rows + 2 * lag_span
    local_count = row_count // tile_rows
    ahead_row = jnp.concatenate(
        [
            jnp.zeros((head_here, 1), kernel.dtype),
            kernel[:, ::-1],
            jnp.zeros((head_here, 2 * tile_rows - 1), kernel.dtype),
        ],
        axis=1,
    )
    behind_row = jnp.concatenate(
        [kernel, jnp.zeros((head_here, 2 * tile_rows), kernel.dtype)], axis=1
    )
    forward_band = banded(ahead_row, tile_rows, window_len)
    value_heads = value_acts.reshape(row_count, head_here, head_width).transpose(1, 2, 0)
    padded = jnp.pad(value_heads, ((0, 0), (0, 0), (2 * lag_span, 2 * lag_span)))
    spread_count = (row_count + 2 * lag_span) // tile_rows
    value_win = windows(padded, tile_rows, spread_count, slot_count)
    spread = jnp.einsum(
        "haw,hcpw->hcpa", forward_band, value_win, preferred_element_type=jnp.float32
    ).reshape(head_here, head_width, row_count + 2 * lag_span)
    from_below = from_behind(
        spread[:, :, row_count + lag_span :].astype(jnp.bfloat16), "seq", 1
    ).astype(jnp.float32)
    from_above = from_behind(spread[:, :, :lag_span].astype(jnp.bfloat16), "seq", -1).astype(
        jnp.float32
    )
    mixed_heads = spread[:, :, lag_span : lag_span + row_count] + from_below + from_above
    mixed_sum = mixed_heads.transpose(2, 0, 1).reshape(row_count, chan_width)
    hidden = gate_acts.astype(jnp.float32) * mixed_sum
    squares = jnp.sum(hidden * hidden, axis=1)
    weighted = norm_gain[None, :] * out_grad.astype(jnp.float32)
    squares = lax.psum(squares, "chan")
    scale = lax.rsqrt(squares / D + norm_eps)
    normed = (hidden * scale[:, None] * norm_gain[None, :]).astype(jnp.bfloat16)
    inner = lax.psum(jnp.sum(weighted * hidden, axis=1), "chan")
    hidden_grad = scale[:, None] * (weighted - hidden * (scale * scale * inner / D)[:, None])
    gate_grad = (hidden_grad * mixed_sum).astype(jnp.bfloat16)
    mix_grad = (hidden_grad * gate_acts.astype(jnp.float32)).astype(jnp.bfloat16)
    gain_local = jnp.sum(out_grad.astype(jnp.float32) * hidden * scale[:, None], axis=0)
    mix_heads = mix_grad.reshape(row_count, head_here, head_width).transpose(1, 2, 0)
    grad_outer = extended_2(mix_heads, (("seq", 2),), lag_span)
    grad_win = windows(grad_outer, tile_rows, local_count, slot_count)
    backward_band = banded(behind_row, tile_rows, window_len)
    value_sum = jnp.einsum(
        "haw,hcpw->hcpa", backward_band, grad_win, preferred_element_type=jnp.float32
    )
    value_grad = (
        value_sum.reshape(head_here, head_width, row_count)
        .transpose(2, 0, 1)
        .reshape(row_count, chan_width)
        .astype(jnp.bfloat16)
    )
    value_tiles = value_heads.reshape(head_here, head_width, local_count, tile_rows)
    cross = jnp.einsum("hcpa,hcpw->haw", value_tiles, grad_win, preferred_element_type=jnp.float32)
    kernel_local = diagonal_sums(cross, 2 * lag_span)
    kernel_total, gain_total = lax.psum((kernel_local, gain_local), "seq")
    tokens = row_count * lax.axis_size("seq")
    kernel_grad = kernel_total / math.sqrt(tokens * head_width)
    gain_grad = gain_total / math.sqrt(tokens)
    return (normed, gate_grad, value_grad, kernel_grad, gain_grad)


def solution(mesh):
    placed = (P("seq", "chan"), P("seq", "chan"), P("chan", None), P("chan"), P("seq", "chan"))
    return jax.shard_map(
        on_device,
        mesh=mesh,
        in_specs=placed,
        out_specs=(
            P("seq", "chan"),
            P("seq", "chan"),
            P("seq", "chan"),
            P("chan", None),
            P("chan"),
        ),
        check_vma=False,
    )
```

profile of v0, /device:TPU:8, one launch (start us, length us, event | category | flops | bytes accessed | tf_op | source)
XLA Modules:
  0.0 578.5 jit_solution(12516928368072669835)
XLA Ops:
  0.6 1.2 copy.11
  1.9 0.8 copy-done.9
  2.7 1.8 pad.5
  4.5 4.2 reshape.59
  8.7 8.3 %fusion.16 = (bf16[4,64,12,256]{3,2,1,0:T(8,128)(2,1)}, bf16[4,64,12,256]{3,2,1,0:T(8,128)(2,1)}, bf16[4,64,12,256]{3,2,1,0:T(8,128)(2,1)}, bf16[4,64,12,256]{3,...) fusion(bf16[4,64,20,256]{3,2,1,0:T(8,128)(2,1)S(1)} %reshape.59), kind=kLoop, calls=%fused_computation.54 | loop fusion | bytes 28311552 | tf_op jit(solution)/shard_map/slice | solution.py:47
  16.9 1.8 copy_dynamic-update-slice_fusion.8
  18.7 1.4 rev.3
  20.2 0.1 concatenate.16
  20.3 0.4 broadcast_bitcast_fusion.1
  20.7 4.0 copy.62
  24.7 4.3 slice.123
  29.1 6.7 %reshape.74 = bf16[2620416]{0:T(1024)(128)(2,1)} reshape(bf16[4,655104]{1,0:T(4,128)(2,1)} %slice.123) | data formatting | bytes 10481664
  35.8 13.0 %reshape.61 = bf16[4,256,2559]{2,1,0:T(8,128)(2,1)} reshape(bf16[2620416]{0:T(1024)(128)(2,1)} %reshape.74) | data formatting | bytes 10481664 | tf_op jit(solution)/shard_map/reshape | solution.py:39
  48.7 3.6 copy_dynamic-update-slice_fusion.7
  52.4 1.7 copy_dynamic-update-slice_fusion.6
  54.1 1.9 copy_dynamic-update-slice_fusion.5
  56.0 1.9 copy_dynamic-update-slice_fusion.4
  57.8 1.8 copy_dynamic-update-slice_fusion.3
  59.6 2.3 copy_dynamic-update-slice_fusion.2
  61.9 1.8 copy_dynamic-update-slice_fusion.1
  63.7 1.8 copy_dynamic-update-slice_fusion
  65.5 10.5 %fusion.2 = f32[4,12,8,8,256]{4,3,2,1,0:T(8,128)} fusion(bf16[4,64,12,2304]{3,1,2,0:T(8,128)(2,1)} %copy_dynamic-update-slice_fusion, bf16[4,256,2559]{2,1,0:T(8,128)(2,1)S(1)} %bitcast.79), kind=kOutput, calls=%fused_computation.8 | convolution fusion | flops 3623878656 | bytes 22020096 | tf_op jit(solution)/shard_map/haw,hcpw->hcpa/dot_general | solution.py:89
  76.0 2.3 copy.60
  78.3 0.2 convert.4
  78.5 1.0 fusion.18
  79.6 3.4 collective-permute-start
  83.0 11.6 %collective-permute-start.1 = (bf16[4,64,1024]{2,1,0:T(8,128)(2,1)}, bf16[4,64,1024]{2,1,0:T(8,128)(2,1)}, u32[]{:S(2)}, u32[]{:S(2)}) collective-permute-start(bf16[4,64,1024]{2,1,0:T(8,128)(2,1)} %get-tuple-element.36), channel_id=1, source_target_pairs={{8,0},{16,8},{24,16},{32,24},{40,32},{48,40},{56,48},{64,56},{72,6... | collective-permute-start | bytes 1572872 | tf_op jit(solution)/shard_map/ppermute | solution.py:18
  94.6 2.0 copy.10
  96.6 2.0 copy.22
  98.6 6.2 %collective-permute-done = bf16[4,64,1024]{2,1,0:T(8,128)(2,1)} collective-permute-done((bf16[4,64,1024]{2,1,0:T(8,128)(2,1)}, bf16[4,64,1024]{2,1,0:T(8,128)(2,1)}, u32[]{:S(2)}, u32[]{:S(2)}) %collective-permute-start) | collective-permute-done | bytes 524320 | tf_op jit(solution)/shard_map/ppermute | solution.py:18
  104.8 1.2 collective-permute-done.1
  106.0 1.4 fusion.12
  107.5 1.0 copy-done
  108.4 1.3 multiply_reduce_fusion
  109.7 17.0 %psum.28 = f32[1024]{0:T(1024)S(1)} all-reduce(f32[1024]{0:T(1024)S(1)} %multiply_reduce_fusion), channel_id=1, replica_groups=mesh['seq'=64,'chan'=8] {'chan'}, use_global_device_ids=true, to_apply=%region_1.2 | all-reduce | flops 1024 | bytes 8192 | tf_op jit(solution)/shard_map/psum | solution.py:103
  126.7 1.9 fusion.11
  128.7 14.2 %psum.29 = f32[1024]{0:T(1024)S(1)} all-reduce(f32[1024]{0:T(1024)S(1)} %get-tuple-element.11), channel_id=1, replica_groups=mesh['seq'=64,'chan'=8] {'chan'}, use_global_device_ids=true, to_apply=%region_3.4 | all-reduce | flops 1024 | bytes 8192 | tf_op jit(solution)/shard_map/psum | solution.py:106
  142.9 2.1 fusion.9
  145.0 1.9 collective-permute-start.2
  147.0 8.6 %collective-permute-start.3 = (bf16[4,64,1024]{2,1,0:T(8,128)(2,1)S(1)}, bf16[4,64,1024]{2,1,0:T(8,128)(2,1)S(1)}, u32[]{:S(2)}, u32[]{:S(2)}) collective-permute-start(bf16[4,64,1024]{2,1,0:T(8,128)(2,1)S(1)} %bitcast.84), channel_id=1, source_target_pairs={{8,0},{16,8},{24,16},{32,24},{40,32},{48,40},{56,48},{64,56},{72,6... | collective-permute-start | bytes 1572872 | tf_op jit(solution)/shard_map/ppermute | solution.py:29
  155.6 0.4 broadcast_bitcast_fusion
  156.0 4.0 copy.63
  160.1 4.3 slice.137
  164.3 6.8 %reshape.76 = bf16[2620416]{0:T(1024)(128)(2,1)} reshape(bf16[4,655104]{1,0:T(4,128)(2,1)} %slice.137) | data formatting | bytes 10481664
  171.2 12.8 %reshape.67 = bf16[4,256,2559]{2,1,0:T(8,128)(2,1)} reshape(bf16[2620416]{0:T(1024)(128)(2,1)} %reshape.76) | data formatting | bytes 10481664 | tf_op jit(solution)/shard_map/reshape | solution.py:39
  184.0 1.0 copy.35
  185.0 1.0 copy.36
  186.0 1.3 pad_maximum_fusion
  187.3 2.9 reshape.65
  190.1 2.7 fusion.17
  193.6 2.2 copy-done.8
  195.8 5.5 convolution_bitcast_fusion
  201.3 9.6 %copy.34 = f32[4,256,2304]{2,1,0:T(8,128)} copy(f32[4,256,2304]{1,2,0:T(8,128)} %convolution_bitcast_fusion) | data formatting | bytes 18874368 | tf_op jit(solution)/shard_map/hcpa,hcpw->haw/dot_general | solution.py:125
  210.9 13.4 %copy.64 = f32[1,4,256,2304]{3,1,2,0:T(4,128)} copy(f32[1,4,256,2304]{3,2,1,0:T(8,128)} %bitcast.73) | data formatting | bytes 18874368
  224.3 9.4 %slice.139 = f32[4,587775]{1,0:T(4,128)} slice(f32[4,589824]{1,0:T(4,128)} %bitcast.71), slice={[0:4], [0:587775]} | slice | bytes 18808800 | tf_op jit(solution)/shard_map/slice | solution.py:58
  233.6 13.1 %reshape.78 = f32[2351100]{0:T(1024)} reshape(f32[4,587775]{1,0:T(4,128)} %slice.139) | data formatting | bytes 18808800
  246.7 14.6 %reshape.70 = f32[4,255,2305]{2,1,0:T(8,128)} reshape(f32[2351100]{0:T(1024)} %reshape.78) | data formatting | bytes 18808800 | tf_op jit(solution)/shard_map/reshape | solution.py:58
  261.3 3.9 slice_reduce_fusion
  265.2 0.8 slice_add_fusion.1
  266.1 304.8 %all-reduce.2 = (f32[4,2048]{1,0:T(4,128)S(1)}, f32[256]{0:T(256)S(1)}) all-reduce(f32[4,2048]{1,0:T(4,128)S(1)} %slice_add_fusion.1, f32[256]{0:T(256)S(1)} %get-tuple-element.10), channel_id=1, replica_groups=mesh['seq'=64,'chan'=8] {'seq'}, use_global_device_ids=true, to_apply=%region_5.6 | all-reduce | flops 8448 | bytes 67584 | tf_op jit(solution)/shard_map/psum | solution.py:127
  570.9 0.6 broadcast_multiply_fusion
  571.5 0.6 broadcast_multiply_fusion.1
  572.1 5.2 fusion.6
  577.3 1.0 copy.37
  (45 shorter events, 0.9 us)
Async XLA Ops:
  1.9 0.8 copy-start.9
  8.6 10.1 %copy-start.11 = (bf16[4,2048]{1,0:T(4,128)(2,1)S(1)}, bf16[4,2048]{1,0:T(4,128)(2,1)}, u32[]{:S(2)}) copy-start(bf16[4,2048]{1,0:T(4,128)(2,1)} %param.7) | copy-start | bytes 49156
  35.8 16.6 %copy-start.7 = (bf16[4,64,12,256]{3,2,1,0:T(8,128)(2,1)S(1)}, bf16[4,64,12,256]{3,2,1,0:T(8,128)(2,1)}, u32[]{:S(2)}) copy-start(bf16[4,64,12,256]{3,2,1,0:T(8,128)(2,1)} %get-tuple-element.20) | copy-start | bytes 4718596
  48.7 5.3 copy-start.6
  48.7 7.2 %copy-start.5 = (bf16[4,64,12,256]{3,2,1,0:T(8,128)(2,1)S(1)}, bf16[4,64,12,256]{3,2,1,0:T(8,128)(2,1)}, u32[]{:S(2)}) copy-start(bf16[4,64,12,256]{3,2,1,0:T(8,128)(2,1)} %get-tuple-element.18) | copy-start | bytes 4718596
  52.4 5.5 copy-start.4
  54.1 5.5 copy-start.3
  56.0 6.0 %copy-start.2 = (bf16[4,64,12,256]{3,2,1,0:T(8,128)(2,1)S(1)}, bf16[4,64,12,256]{3,2,1,0:T(8,128)(2,1)}, u32[]{:S(2)}) copy-start(bf16[4,64,12,256]{3,2,1,0:T(8,128)(2,1)} %get-tuple-element.15) | copy-start | bytes 4718596
  56.0 9.5 %slice-start = ((s8[5242880]{0:T(1024)(128)(4,1)}), s8[4194304]{0:T(1024)(128)(4,1)S(1)}, s32[]{:S(2)}) async-start(s8[5242880]{0:T(1024)(128)(4,1)} %bitcast.78), calls=%async_computation | async-start | bytes 8388608
  57.8 5.9 %copy-start.1 = (bf16[4,64,12,256]{3,2,1,0:T(8,128)(2,1)S(1)}, bf16[4,64,12,256]{3,2,1,0:T(8,128)(2,1)}, u32[]{:S(2)}) copy-start(bf16[4,64,12,256]{3,2,1,0:T(8,128)(2,1)} %get-tuple-element.14) | copy-start | bytes 4718596
  59.6 5.9 %slice-start.1 = ((s8[5242880]{0:T(1024)(128)(4,1)}), s8[1048576]{0:T(1024)(128)(4,1)S(1)}, s32[]{:S(2)}) async-start(s8[5242880]{0:T(1024)(128)(4,1)} %bitcast.78), calls=%async_computation.1 | async-start | bytes 2097152
  78.5 48.2 %copy-start.12 = (f32[256]{0:T(256)S(1)}, f32[256]{0:T(256)}, u32[]{:S(2)}) copy-start(f32[256]{0:T(256)} %param.8) | copy-start | bytes 3076
  79.6 25.2 %collective-permute-start = (bf16[4,64,1024]{2,1,0:T(8,128)(2,1)}, bf16[4,64,1024]{2,1,0:T(8,128)(2,1)}, u32[]{:S(2)}, u32[]{:S(2)}) collective-permute-start(bf16[4,64,1024]{2,1,0:T(8,128)(2,1)} %get-tuple-element.35), channel_id=1, source_target_pairs={{0,8},{8,16},{16,24},{24,32},{32,40},{40,48},{48,56},{56,64},{64,7... | collective-permute-start | bytes 1572872 | tf_op jit(solution)/shard_map/ppermute | solution.py:18
  83.0 23.0 %collective-permute-start.1 = (bf16[4,64,1024]{2,1,0:T(8,128)(2,1)}, bf16[4,64,1024]{2,1,0:T(8,128)(2,1)}, u32[]{:S(2)}, u32[]{:S(2)}) collective-permute-start(bf16[4,64,1024]{2,1,0:T(8,128)(2,1)} %get-tuple-element.36), channel_id=1, source_target_pairs={{8,0},{16,8},{24,16},{32,24},{40,32},{48,40},{56,48},{64,56},{72,6... | collective-permute-start | bytes 1572872 | tf_op jit(solution)/shard_map/ppermute | solution.py:18
  107.4 1.0 copy-start
  145.0 40.9 %collective-permute-start.2 = (bf16[4,64,1024]{2,1,0:T(8,128)(2,1)S(1)}, bf16[4,64,1024]{2,1,0:T(8,128)(2,1)S(1)}, u32[]{:S(2)}, u32[]{:S(2)}) collective-permute-start(bf16[4,64,1024]{2,1,0:T(8,128)(2,1)S(1)} %bitcast.83), channel_id=1, source_target_pairs={{0,8},{8,16},{16,24},{24,32},{32,40},{40,48},{48,56},{56,64},{64,7... | collective-permute-start | bytes 1572872 | tf_op jit(solution)/shard_map/ppermute | solution.py:26
  147.0 39.0 %collective-permute-start.3 = (bf16[4,64,1024]{2,1,0:T(8,128)(2,1)S(1)}, bf16[4,64,1024]{2,1,0:T(8,128)(2,1)S(1)}, u32[]{:S(2)}, u32[]{:S(2)}) collective-permute-start(bf16[4,64,1024]{2,1,0:T(8,128)(2,1)S(1)} %bitcast.84), channel_id=1, source_target_pairs={{8,0},{16,8},{24,16},{32,24},{40,32},{48,40},{56,48},{64,56},{72,6... | collective-permute-start | bytes 1572872 | tf_op jit(solution)/shard_map/ppermute | solution.py:29
  192.8 3.0 copy-start.10
  193.6 2.2 copy-start.8
where the time goes:
time: 587 us; the launch traced here: 578 us
  blocking collectives  336 us (57%)
  local copies, waits for them, and re-layouts  173 us (29%)
  starting transfers between devices  25.5 us (4%)
  matrix products  21.1 us (4%)
  other arithmetic  14.2 us (2%)
  waiting for transfers between devices  7.37 us (1%)
    psum x1, blocking collectives, on_device(): kernel_total, gain_total = lax.psum((kernel_local, gain_local), 'seq')  305 us
    unnamed x60, local copies, waits for them, and re-layouts  78.6 us
    reshape x2, local copies, waits for them, and re-layouts, banded(): flat_rows.reshape(head_here, tile_rows, row_full - 1)[:, :, :window_len]  25.8 us
    psum x1, blocking collectives, on_device(): squares = lax.psum(squares, 'chan')  17 us
    ppermute x2, starting transfers between devices, from_behind(): return lax.ppermute(value, axis, pairs)  14.9 us
    reshape x1, local copies, waits for them, and re-layouts, diagonal_sums(): flat_rows[:, :cut_at].reshape(head_here, tile_rows - 1, window_len + 1)  14.6 us
    psum x1, blocking collectives, on_device(): inner = lax.psum(jnp.sum(weighted * hidden, axis=1), 'chan')  14.2 us
  transfers between devices with their start and end apart: 4, of which 2 were waited for; matrix products, arithmetic and copies ran while one was open for 6% of the time, Pallas kernels for 0%

commit v1 on v0

v1 whole, which is shorter than its diff:
```python
import functools
import math

import jax
import jax.numpy as jnp
from jax import lax
from jax.experimental import pallas as pl
from jax.experimental.pallas import tpu as pltpu
from jax.sharding import PartitionSpec as P

EPS = 1e-06
ROWS = 1024
WIDTH = 256
TILE = 256
HEADS = 4
SLOTS = 9
SPAN = 2432
F32 = jnp.float32
BF16 = jnp.bfloat16
MESH = pl.DeviceIdType.MESH


def tile_at(t):
    return pl.ds(t * TILE, TILE)


def build_band(row, first, band, h):
    wide = jnp.concatenate(
        [jnp.broadcast_to(row, (8, 2048)), jnp.zeros((8, SPAN - 2048), F32)], axis=1
    )
    sub = lax.broadcasted_iota(jnp.int32, (8, SPAN), 0)
    if first:
        wide = pltpu.roll(wide, first, 1)
    for bit in (1, 2, 4):
        wide = jnp.where((sub & bit) != 0, pltpu.roll(wide, bit, 1), wide)
    base = jnp.concatenate([wide, pltpu.roll(wide, 8, 1)], axis=0)
    for g in range(8):
        part = (pltpu.roll(base, 16 * g, 1) if g else base).astype(BF16)
        low = jnp.concatenate([jnp.zeros((16, 128), BF16), part[:, : SPAN - 256]], axis=1)
        for s in range(SLOTS):
            band[h, s, 16 * g : 16 * g + 16, :] = part[:, 256 * s : 256 * s + 256]
            band[h, s, 128 + 16 * g : 144 + 16 * g, :] = low[:, 256 * s : 256 * s + 256]


def swap_halves(x):
    return jnp.concatenate([x[:, 64:], x[:, :64]], axis=1)


def make_pair(ext, pairs, t):
    low = lax.broadcasted_iota(jnp.int32, (TILE, 128), 1) < 64
    for hp in range(2):
        a = ext[tile_at(t), 128 * hp : 128 * hp + 128]
        b = ext[tile_at(t + 1), 128 * hp : 128 * hp + 128]
        pairs[2 * hp, t] = jnp.where(low, a, swap_halves(b))
        pairs[2 * hp + 1, t] = jnp.where(low, swap_halves(a), b)


def add_slots(band, pairs, total, slots, fresh=False):
    def one(h, carry):
        acc = None
        for s in slots:
            right = jnp.concatenate([pairs[h, s], pairs[h, s + 2]], axis=1)
            term = jnp.dot(band[h, s], right, preferred_element_type=F32)
            acc = term if acc is None else acc + term
        total[h] = acc if fresh else total[h] + acc
        return carry

    lax.fori_loop(0, HEADS, one, 0)


def to_rows(total, out, dtype):
    low = lax.broadcasted_iota(jnp.int32, (TILE, 128), 1) < 64
    for hp in range(2):
        for pp in range(2):
            a = total[2 * hp, :, 128 * pp : 128 * pp + 128]
            b = total[2 * hp + 1, :, 128 * pp : 128 * pp + 128]
            lanes = slice(128 * hp, 128 * hp + 128)
            out[tile_at(2 * pp), lanes] = jnp.where(low, a, swap_halves(b)).astype(dtype)
            out[tile_at(2 * pp + 1), lanes] = jnp.where(low, swap_halves(a), b).astype(dtype)


def kernel_body(
    dims,
    chans,
    gate_in,
    value_in,
    taps_ref,
    gain_ref,
    grad_in,
    normed_out,
    gate_grad_out,
    value_grad_out,
    taps_grad_ref,
    gain_grad_ref,
    vext,
    mext,
    gate_ref,
    grad_ref,
    ahead,
    behind,
    vpairs,
    mpairs,
    total,
    mixed,
    normed_ref,
    gate_grad_ref,
    value_grad_ref,
    lag_sum,
    chan_buf,
    row_scale,
    gain_sum,
    cut_src,
    cut_buf,
    all_buf,
    gather_buf,
    load_sem,
    store_sem,
    vsend,
    vrecv,
    msend,
    mrecv,
    chan_send,
    chan_recv,
    cut_send,
    cut_recv,
    all_send,
    all_recv,
    gather_send,
    gather_recv,
):
    ny, nz, nx = dims
    nseq = ny * nz * nx
    nq = ny * nx
    cut = 64 // nz
    depth = WIDTH * chans
    me = lax.axis_index("seq")
    ch = lax.axis_index("chan")
    x = lax.rem(me, nx)
    z = lax.rem(lax.div(me, nx), nz)
    y = lax.div(me, nx * nz)
    q = y * nx + x
    has_prev = me > 0
    has_next = me < nseq - 1
    prev_dev = (lax.rem(me + nseq - 1, nseq), ch)
    next_dev = (lax.rem(me + 1, nseq), ch)

    def chan_dev(j):
        return (me, lax.rem(ch + j, chans))

    def z_of(j):
        return lax.rem(z + j, nz)

    def z_dev(j):
        return ((y * nz + z_of(j)) * nx + x, ch)

    def q_dev(j):
        other = lax.rem(q + j, nq)
        return ((lax.div(other, nx) * nz + z) * nx + lax.rem(other, nx), ch)

    barrier = pltpu.get_barrier_semaphore()
    partners = (
        [prev_dev, next_dev]
        + [chan_dev(j) for j in range(1, chans)]
        + [z_dev(j) for j in range(1, nz)]
        + [q_dev(j) for j in range(1, nq)]
    )
    for dev in partners:
        pl.semaphore_signal(barrier, inc=1, device_id=dev, device_id_type=MESH)

    loads = [
        pltpu.make_async_copy(value_in, vext.at[pl.ds(ROWS, ROWS)], load_sem.at[0]),
        pltpu.make_async_copy(gate_in, gate_ref, load_sem.at[1]),
        pltpu.make_async_copy(grad_in, grad_ref, load_sem.at[2]),
    ]
    for load in loads:
        load.start()
    pl.semaphore_wait(barrier, len(partners))

    def to_next(src, ext, send, recv, t):
        return pltpu.make_async_remote_copy(
            src_ref=src,
            dst_ref=ext.at[tile_at(t)],
            send_sem=send.at[0, t],
            recv_sem=recv.at[0, t],
            device_id=next_dev,
            device_id_type=MESH,
        )

    def to_prev(src, ext, send, recv, t):
        return pltpu.make_async_remote_copy(
            src_ref=src,
            dst_ref=ext.at[tile_at(8 + t)],
            send_sem=send.at[1, t],
            recv_sem=recv.at[1, t],
            device_id=prev_dev,
            device_id_type=MESH,
        )

    v_next = [to_next(value_in.at[tile_at(t)], vext, vsend, vrecv, t) for t in range(4)]
    v_prev = [to_prev(value_in.at[tile_at(t)], vext, vsend, vrecv, t) for t in range(4)]
    m_next = [to_next(mext.at[tile_at(4 + t)], mext, msend, mrecv, t) for t in range(4)]
    m_prev = [to_prev(mext.at[tile_at(4 + t)], mext, msend, mrecv, t) for t in range(4)]

    @pl.when(has_next)
    def _():
        for t in (3, 2, 1, 0):
            v_next[t].start()

    @pl.when(has_prev)
    def _():
        for t in range(4):
            v_prev[t].start()

    @pl.when(jnp.logical_not(has_prev))
    def _():
        vext[0:ROWS, :] = jnp.zeros((ROWS, WIDTH), BF16)
        mext[0:ROWS, :] = jnp.zeros((ROWS, WIDTH), BF16)

    @pl.when(jnp.logical_not(has_next))
    def _():
        vext[2 * ROWS : 3 * ROWS, :] = jnp.zeros((ROWS, WIDTH), BF16)
        mext[2 * ROWS : 3 * ROWS, :] = jnp.zeros((ROWS, WIDTH), BF16)

    taps = jnp.concatenate([taps_ref[...].astype(F32), jnp.zeros((4, 2048), F32)], axis=0)
    stacked = jnp.concatenate([taps[:, 128 * b : 128 * b + 128] for b in range(16)], axis=0)
    flip = (
        lax.broadcasted_iota(jnp.int32, (128, 128), 0)
        + lax.broadcasted_iota(jnp.int32, (128, 128), 1)
        == 127
    ).astype(BF16)
    turned = jnp.dot(stacked.astype(BF16), flip, preferred_element_type=F32)
    back = jnp.concatenate([turned[8 * b : 8 * b + 8] for b in reversed(range(16))], axis=1)
    for h in range(HEADS):
        build_band(back[h : h + 1], 1, ahead, h)
    loads[0].wait()
    for t in (4, 5, 6):
        make_pair(vext, vpairs, t)
    add_slots(ahead, vpairs, total, [4], fresh=True)
    for h in range(HEADS):
        build_band(taps[h : h + 1], 0, behind, h)

    def arrive(ext, pairs, band, nexts, prevs, c):
        @pl.when(has_prev)
        def _():
            nexts[4 - c].wait_recv()

        @pl.when(has_next)
        def _():
            prevs[c - 1].wait_recv()

        make_pair(ext, pairs, 4 - c)
        make_pair(ext, pairs, 6 + c)
        add_slots(band, pairs, total, [4 - c, 4 + c])

    loads[1].wait()
    loads[2].wait()
    for c in range(1, 5):
        arrive(vext, vpairs, ahead, v_next, v_prev, c)
    to_rows(total, mixed, F32)

    gain = gain_ref[...]

    def block_at(b):
        return pl.ds(pl.multiple_of(b * 128, 128), 128)

    def sums(b, carry):
        rows = block_at(b)
        hidden = gate_ref[rows, :].astype(F32) * mixed[rows, :]
        square = hidden * hidden
        inner = gain * grad_ref[rows, :].astype(F32) * hidden
        for k, v in ((0, square), (8, inner)):
            half = (v[:, :128] + v[:, 128:]).T
            chan_buf[ch, pl.ds(k + b, 1), :] = jnp.sum(half, axis=0, keepdims=True)
        return carry

    lax.fori_loop(0, 8, sums, 0)

    def exchange(src_of, dst, send, recv, dev_of, count):
        return [
            pltpu.make_async_remote_copy(
                src_ref=src_of(j),
                dst_ref=dst,
                send_sem=send.at[j],
                recv_sem=recv.at[j],
                device_id=dev_of(j),
                device_id_type=MESH,
            )
            for j in range(1, count)
        ]

    chan_copies = exchange(
        lambda j: chan_buf.at[ch], chan_buf.at[ch], chan_send, chan_recv, chan_dev, chans
    )
    for copy in chan_copies:
        copy.start()
    for copy in chan_copies:
        copy.wait_recv()
    sums_all = chan_buf[0]
    for j in range(1, chans):
        sums_all = sums_all + chan_buf[j]
    scale = lax.rsqrt(sums_all[0:8] / depth + EPS)
    row_scale[0:8, :] = scale
    row_scale[8:16, :] = scale * scale * sums_all[8:16] / depth
    gain_sum[...] = jnp.zeros((8, WIDTH), F32)

    def apply(b, carry):
        rows = block_at(b)

        def column(k):
            tall = jnp.broadcast_to(row_scale[pl.ds(k + b, 1), :], (128, 128)).T
            return jnp.concatenate([tall, tall], axis=1)

        scale = column(0)
        pull = column(8)
        gate = gate_ref[rows, :].astype(F32)
        grad = grad_ref[rows, :].astype(F32)
        mix = mixed[rows, :]
        hidden = gate * mix
        scaled = hidden * scale
        normed_ref[rows, :] = (scaled * gain).astype(BF16)
        hidden_grad = scale * (gain * grad - hidden * pull)
        gate_grad_ref[rows, :] = (hidden_grad * mix).astype(BF16)
        mext[pl.ds(pl.multiple_of(ROWS + b * 128, 128), 128), :] = (hidden_grad * gate).astype(BF16)
        term = grad * scaled
        gain_sum[...] += jnp.sum(term.reshape(16, 8, WIDTH), axis=0)
        return carry

    def apply_tile(t):
        lax.fori_loop(2 * t, 2 * t + 2, apply, 0)

    def send_next(*tiles):
        @pl.when(has_next)
        def _():
            for t in tiles:
                m_next[t].start()

    def send_prev(*tiles):
        @pl.when(has_prev)
        def _():
            for t in tiles:
                m_prev[t].start()

    apply_tile(0)
    send_prev(0)
    apply_tile(3)
    send_next(3)
    apply_tile(1)
    send_prev(1)
    apply_tile(2)
    send_next(2, 1, 0)
    send_prev(2, 3)
    stores = [
        pltpu.make_async_copy(normed_ref, normed_out, store_sem.at[0]),
        pltpu.make_async_copy(gate_grad_ref, gate_grad_out, store_sem.at[1]),
        pltpu.make_async_copy(value_grad_ref, value_grad_out, store_sem.at[2]),
    ]
    stores[0].start()
    stores[1].start()

    for t in (4, 5, 6):
        make_pair(mext, mpairs, t)

    def lag_terms(h, carry):
        lag_sum[...] = jnp.zeros((128, SPAN), F32)
        local = jnp.concatenate([mpairs[h, 4], mpairs[h, 6]], axis=1)
        for s in range(SLOTS):
            window = jnp.concatenate([vpairs[h, s], vpairs[h, s + 2]], axis=1)
            cross = lax.dot_general(
                window, local, (((1,), (1,)), ((), ())), preferred_element_type=F32
            )
            for k in range(2):
                at = (17 - 2 * s - k) * 128
                lag_sum[:, at : at + 256] += cross[128 * k : 128 * k + 128]
        eight = lag_sum[0:8, :]
        for g in range(1, 16):
            eight = eight + pltpu.roll(lag_sum[8 * g : 8 * g + 8, :], SPAN - 8 * g, 1)
        sub = lax.broadcasted_iota(jnp.int32, (8, SPAN), 0)
        for bit in (1, 2, 4):
            eight = jnp.where((sub & bit) != 0, pltpu.roll(eight, SPAN - bit, 1), eight)
        line = jnp.sum(eight, axis=0, keepdims=True)
        for b in range(16):
            row = h * 16 + b
            cut_src[lax.div(row, cut), pl.ds(lax.rem(row, cut), 1), :] = line[
                :, 128 + 128 * b : 256 + 128 * b
            ]
        return carry

    lax.fori_loop(0, HEADS, lag_terms, 0)
    gains = jnp.sum(gain_sum[...], axis=0, keepdims=True)
    gain_rows = jnp.concatenate(
        [gains[:, :128], gains[:, 128:], jnp.zeros((6, 128), F32)], axis=0
    )
    for k in range(nz):
        cut_src[k, cut : cut + 8, :] = gain_rows

    cut_copies = exchange(
        lambda j: cut_src.at[z_of(j)], cut_buf.at[z], cut_send, cut_recv, z_dev, nz
    )
    for copy in cut_copies:
        copy.start()
    cut_buf[z] = cut_src[z]

    add_slots(behind, mpairs, total, [4], fresh=True)
    for copy in cut_copies:
        copy.wait_recv()
    part = cut_buf[0]
    for k in range(1, nz):
        part = part + cut_buf[k]
    all_buf[q] = part
    all_copies = exchange(lambda j: all_buf.at[q], all_buf.at[q], all_send, all_recv, q_dev, nq)
    for copy in all_copies:
        copy.start()
    arrive(mext, mpairs, behind, m_next, m_prev, 1)
    for copy in all_copies:
        copy.wait_recv()
    part = all_buf[0]
    for k in range(1, nq):
        part = part + all_buf[k]
    gather_buf[z] = part[0:cut] * (1.0 / math.sqrt(ROWS * nseq * 64))
    gather_copies = exchange(
        lambda j: gather_buf.at[z], gather_buf.at[z], gather_send, gather_recv, z_dev, nz
    )
    for copy in gather_copies:
        copy.start()
    gains = jnp.concatenate([part[cut : cut + 1], part[cut + 1 : cut + 2]], axis=1)
    gain_grad_ref[...] = gains * (1.0 / math.sqrt(ROWS * nseq))
    for c in (2, 3, 4):
        arrive(mext, mpairs, behind, m_next, m_prev, c)
    to_rows(total, value_grad_ref, BF16)
    stores[2].start()
    for copy in gather_copies:
        copy.wait_recv()
    for row in range(64):
        h, b = divmod(row, 16)
        k, r = divmod(row, cut)
        taps_grad_ref[h : h + 1, 128 * b : 128 * b + 128] = gather_buf[k, r : r + 1, :]

    for copy in chan_copies + cut_copies + all_copies + gather_copies:
        copy.wait_send()

    @pl.when(has_next)
    def _():
        for t in range(4):
            v_next[t].wait_send()
            m_next[t].wait_send()

    @pl.when(has_prev)
    def _():
        for t in range(4):
            v_prev[t].wait_send()
            m_prev[t].wait_send()

    for store in stores:
        store.wait()


def on_device(dims, chans, gate_acts, value_acts, taps, norm_gain, out_grad):
    ny, nz, nx = dims
    nq = ny * nx
    cut = 64 // nz
    block = jax.ShapeDtypeStruct((ROWS, WIDTH), BF16)
    anywhere = pl.BlockSpec(memory_space=pl.ANY)
    vmem = pl.BlockSpec(memory_space=pltpu.VMEM)
    dma = pltpu.SemaphoreType.DMA
    call = pl.pallas_call(
        functools.partial(kernel_body, dims, chans),
        out_shape=(
            block,
            block,
            block,
            jax.ShapeDtypeStruct((HEADS, 2048), F32),
            jax.ShapeDtypeStruct((1, WIDTH), F32),
        ),
        in_specs=[anywhere, anywhere, vmem, vmem, anywhere],
        out_specs=(anywhere, anywhere, anywhere, vmem, vmem),
        scratch_shapes=[
            pltpu.VMEM((3 * ROWS, WIDTH), BF16),
            pltpu.VMEM((3 * ROWS, WIDTH), BF16),
            pltpu.VMEM((ROWS, WIDTH), BF16),
            pltpu.VMEM((ROWS, WIDTH), BF16),
            pltpu.VMEM((HEADS, SLOTS, TILE, TILE), BF16),
            pltpu.VMEM((HEADS, SLOTS, TILE, TILE), BF16),
            pltpu.VMEM((HEADS, 11, TILE, 128), BF16),
            pltpu.VMEM((HEADS, 11, TILE, 128), BF16),
            pltpu.VMEM((HEADS, TILE, TILE), F32),
            pltpu.VMEM((ROWS, WIDTH), F32),
            pltpu.VMEM((ROWS, WIDTH), BF16),
            pltpu.VMEM((ROWS, WIDTH), BF16),
            pltpu.VMEM((ROWS, WIDTH), BF16),
            pltpu.VMEM((128, SPAN), F32),
            pltpu.VMEM((chans, 16, 128), F32),
            pltpu.VMEM((16, 128), F32),
            pltpu.VMEM((8, WIDTH), F32),
            pltpu.VMEM((nz, cut + 8, 128), F32),
            pltpu.VMEM((nz, cut + 8, 128), F32),
            pltpu.VMEM((nq, cut + 8, 128), F32),
            pltpu.VMEM((nz, cut, 128), F32),
            dma((3,)),
            dma((3,)),
            dma((2, 4)),
            dma((2, 4)),
            dma((2, 4)),
            dma((2, 4)),
            dma((chans,)),
            dma((chans,)),
            dma((nz,)),
            dma((nz,)),
            dma((nq,)),
            dma((nq,)),
            dma((nz,)),
            dma((nz,)),
        ],
        compiler_params=pltpu.CompilerParams(
            collective_id=0, has_side_effects=True, vmem_limit_bytes=48 * 1024 * 1024
        ),
        cost_estimate=pl.CostEstimate(
            flops=3_700_000_000, bytes_accessed=6_000_000, transcendentals=1024
        ),
        name="toeplitz_mix",
    )
    normed, gate_grad, value_grad, taps_grad, gain_grad = call(
        gate_acts, value_acts, taps, norm_gain.reshape(1, WIDTH), out_grad
    )
    return normed, gate_grad, value_grad, taps_grad, gain_grad.reshape(WIDTH)


def solution(mesh, dims=(2, 8, 4)):
    placed = (P("seq", "chan"), P("seq", "chan"), P("chan", None), P("chan"), P("seq", "chan"))
    return jax.shard_map(
        functools.partial(on_device, dims, mesh.shape["chan"]),
        mesh=mesh,
        in_specs=placed,
        out_specs=(
            P("seq", "chan"),
            P("seq", "chan"),
            P("seq", "chan"),
            P("chan", None),
            P("chan"),
        ),
        check_vma=False,
    )
```

time: 587 us -> 70.6 us (0.12)
  the two profiles are of different devices: /device:TPU:8 before, /device:TPU:2 now
where the time goes in v1:
time: 70.6 us; the launch traced here: 70.2 us
  Pallas kernels  61.5 us (87%)
  local copies, waits for them, and re-layouts  8.07 us (11%)
    pallas_call x1, Pallas kernels, on_device(): call(gate_acts, value_acts, taps, norm_gain.reshape(1, WIDTH), out_grad)  61.5 us
    unnamed x15, local copies, waits for them, and re-layouts  8.07 us

profile of v1, /device:TPU:2, one launch (start us, length us, event | category | flops | bytes accessed | tf_op | source)
XLA Modules:
  0.0 70.2 jit_solution(12661933532579333949)
XLA Ops:
  0.6 0.0 copy-start.4
  0.6 0.7 copy-done.4
  1.3 0.0 copy-start
  1.3 1.0 %copy-done = bf16[1024,256]{1,0:T(8,128)(2,1)S(1)} copy-done((bf16[1024,256]{1,0:T(8,128)(2,1)S(1)}, bf16[1024,256]{1,0:T(8,128)(2,1)}, u32[]{:S(2)}) %copy-start) | copy-done | bytes 524312
  2.4 0.0 copy-start.1
  2.4 1.0 %copy-done.1 = bf16[1024,256]{1,0:T(8,128)(2,1)S(1)} copy-done((bf16[1024,256]{1,0:T(8,128)(2,1)S(1)}, bf16[1024,256]{1,0:T(8,128)(2,1)}, u32[]{:S(2)}) %copy-start.1) | copy-done | bytes 524312
  3.4 0.0 copy-start.2
  3.4 1.0 %copy-done.2 = bf16[1024,256]{1,0:T(8,128)(2,1)S(1)} copy-done((bf16[1024,256]{1,0:T(8,128)(2,1)S(1)}, bf16[1024,256]{1,0:T(8,128)(2,1)}, u32[]{:S(2)}) %copy-start.2) | copy-done | bytes 524312
  4.4 0.0 copy-start.3
  4.4 0.7 %copy-done.3 = bf16[4,2048]{1,0:T(4,128)(2,1)S(1)} copy-done((bf16[4,2048]{1,0:T(4,128)(2,1)S(1)}, bf16[4,2048]{1,0:T(4,128)(2,1)}, u32[]{:S(2)}) %copy-start.3) | copy-done | bytes 16408
  5.2 61.5 %toeplitz_mix.1 = (bf16[1024,256]{1,0:T(8,128)(2,1)S(1)}, bf16[1024,256]{1,0:T(8,128)(2,1)S(1)}, bf16[1024,256]{1,0:T(8,128)(2,1)S(1)}, f32[4,2048]{1,0:T(4,128)S(1)}, f32[1,256]{1,0:T(1,128)S(1)}) custom-call(bf16[1024,256]{1,0:T(8,128)(2,1)S(1)} %copy-done, bf16[1024,256]{1,0:T(8,128)(2,1)S(1)} %copy-done.1, bf16[4,2048]{1,0:T(4,128)(2,1)S(1)} %copy-done.3, ...), custom_call_target="tpu_custom_call" | custom-call | flops 3700000000 | bytes 6000000 | tf_op jit(solution)/shard_map/toeplitz_mix/pallas_call | solution.py:521
  66.7 0.8 %copy.15 = bf16[1024,256]{1,0:T(8,128)(2,1)} copy(bf16[1024,256]{1,0:T(8,128)(2,1)S(1)} %get-tuple-element.20) | data formatting | bytes 1048576
  67.5 0.8 %copy.16 = bf16[1024,256]{1,0:T(8,128)(2,1)} copy(bf16[1024,256]{1,0:T(8,128)(2,1)S(1)} %get-tuple-element.21) | data formatting | bytes 1048576
  68.3 0.8 %copy.17 = bf16[1024,256]{1,0:T(8,128)(2,1)} copy(bf16[1024,256]{1,0:T(8,128)(2,1)S(1)} %get-tuple-element.22) | data formatting | bytes 1048576
  69.1 0.6 copy.18
  69.7 0.6 copy.19
Async XLA Ops:
  0.6 0.7 copy-start.4
  1.3 1.0 %copy-start = (bf16[1024,256]{1,0:T(8,128)(2,1)S(1)}, bf16[1024,256]{1,0:T(8,128)(2,1)}, u32[]{:S(2)}) copy-start(bf16[1024,256]{1,0:T(8,128)(2,1)} %gate_in.1) | copy-start | bytes 1572868
  2.4 1.0 %copy-start.1 = (bf16[1024,256]{1,0:T(8,128)(2,1)S(1)}, bf16[1024,256]{1,0:T(8,128)(2,1)}, u32[]{:S(2)}) copy-start(bf16[1024,256]{1,0:T(8,128)(2,1)} %value_in.1) | copy-start | bytes 1572868
  3.4 1.0 %copy-start.2 = (bf16[1024,256]{1,0:T(8,128)(2,1)S(1)}, bf16[1024,256]{1,0:T(8,128)(2,1)}, u32[]{:S(2)}) copy-start(bf16[1024,256]{1,0:T(8,128)(2,1)} %grad_in.1) | copy-start | bytes 1572868
  4.4 0.7 %copy-start.3 = (bf16[4,2048]{1,0:T(4,128)(2,1)S(1)}, bf16[4,2048]{1,0:T(4,128)(2,1)}, u32[]{:S(2)}) copy-start(bf16[4,2048]{1,0:T(4,128)(2,1)} %taps_ref.1) | copy-start | bytes 49156

commit v2 on v1

--- a/solution.py
+++ b/solution.py
@@ -18,6 +18,14 @@
 F32 = jnp.float32
 BF16 = jnp.bfloat16
 MESH = pl.DeviceIdType.MESH
+
+
+def far_first(count):
+    return sorted(range(1, count), key=lambda j: -min(j, count - j))
+
+
+def far_first_xy(nx, ny):
+    return sorted(range(1, nx * ny), key=lambda j: -min(j % nx, nx - j % nx))
 
 
 def tile_at(t):
@@ -68,15 +76,30 @@
     lax.fori_loop(0, HEADS, one, 0)
 
 
-def to_rows(total, out, dtype):
+def outer_rows(total, put):
     low = lax.broadcasted_iota(jnp.int32, (TILE, 128), 1) < 64
     for hp in range(2):
-        for pp in range(2):
-            a = total[2 * hp, :, 128 * pp : 128 * pp + 128]
-            b = total[2 * hp + 1, :, 128 * pp : 128 * pp + 128]
-            lanes = slice(128 * hp, 128 * hp + 128)
-            out[tile_at(2 * pp), lanes] = jnp.where(low, a, swap_halves(b)).astype(dtype)
-            out[tile_at(2 * pp + 1), lanes] = jnp.where(low, swap_halves(a), b).astype(dtype)
+        a = total[2 * hp, :, 0:128]
+        b = total[2 * hp + 1, :, 0:128]
+        put(0, hp, jnp.where(low, a, swap_halves(b)))
+        a = total[2 * hp, :, 128:256]
+        b = total[2 * hp + 1, :, 128:256]
+        put(3, hp, jnp.where(low, swap_halves(a), b))
+
+
+def inner_rows(total, extra, put):
+    low = lax.broadcasted_iota(jnp.int32, (TILE, 128), 1) < 64
+    for hp in range(2):
+        more_a = 0.0 if extra is None else extra[2 * hp]
+        more_b = 0.0 if extra is None else extra[2 * hp + 1]
+        swap_a = 0.0 if extra is None else swap_halves(more_a)
+        swap_b = 0.0 if extra is None else swap_halves(more_b)
+        a = total[2 * hp, :, 0:128]
+        b = total[2 * hp + 1, :, 0:128]
+        put(1, hp, jnp.where(low, swap_halves(a) + more_a, b + swap_b))
+        a = total[2 * hp, :, 128:256]
+        b = total[2 * hp + 1, :, 128:256]
+        put(2, hp, jnp.where(low, a + swap_a, swap_halves(b) + more_b))
 
 
 def kernel_body(
@@ -84,8 +107,8 @@
     chans,
     gate_in,
     value_in,
-    taps_ref,
-    gain_ref,
+    taps_in,
+    gain_in,
     grad_in,
     normed_out,
     gate_grad_out,
@@ -96,15 +119,15 @@
     mext,
     gate_ref,
     grad_ref,
+    taps_ref,
+    gain_ref,
     ahead,
     behind,
     vpairs,
     mpairs,
     total,
+    extra,
     mixed,
-    normed_ref,
-    gate_grad_ref,
-    value_grad_ref,
     lag_sum,
     chan_buf,
     row_scale,
@@ -114,7 +137,6 @@
     all_buf,
     gather_buf,
     load_sem,
-    store_sem,
     vsend,
     vrecv,
     msend,
@@ -159,10 +181,10 @@
 
     barrier = pltpu.get_barrier_semaphore()
     partners = (
-        [prev_dev, next_dev]
-        + [chan_dev(j) for j in range(1, chans)]
-        + [z_dev(j) for j in range(1, nz)]
-        + [q_dev(j) for j in range(1, nq)]
+        [z_dev(j) for j in far_first(nz)]
+        + [chan_dev(j) for j in far_first(chans)]
+        + [q_dev(j) for j in far_first_xy(nx, ny)]
+        + [prev_dev, next_dev]
     )
     for dev in partners:
         pl.semaphore_signal(barrier, inc=1, device_id=dev, device_id_type=MESH)
@@ -171,9 +193,11 @@
         pltpu.make_async_copy(value_in, vext.at[pl.ds(ROWS, ROWS)], load_sem.at[0]),
         pltpu.make_async_copy(gate_in, gate_ref, load_sem.at[1]),
         pltpu.make_async_copy(grad_in, grad_ref, load_sem.at[2]),
+        pltpu.make_async_copy(taps_in, taps_ref, load_sem.at[3]),
+        pltpu.make_async_copy(gain_in, gain_ref, load_sem.at[4]),
     ]
-    for load in loads:
-        load.start()
+    for k in (3, 0, 1, 2, 4):
+        loads[k].start()
     pl.semaphore_wait(barrier, len(partners))
 
     def to_next(src, ext, send, recv, t):
@@ -221,6 +245,7 @@
         vext[2 * ROWS : 3 * ROWS, :] = jnp.zeros((ROWS, WIDTH), BF16)
         mext[2 * ROWS : 3 * ROWS, :] = jnp.zeros((ROWS, WIDTH), BF16)
 
+    loads[3].wait()
     taps = jnp.concatenate([taps_ref[...].astype(F32), jnp.zeros((4, 2048), F32)], axis=0)
     stacked = jnp.concatenate([taps[:, 128 * b : 128 * b + 128] for b in range(16)], axis=0)
     flip = (
@@ -239,43 +264,60 @@
     for h in range(HEADS):
         build_band(taps[h : h + 1], 0, behind, h)
 
-    def arrive(ext, pairs, band, nexts, prevs, c):
+    def arrive(nexts, prevs, below, above):
         @pl.when(has_prev)
         def _():
-            nexts[4 - c].wait_recv()
+            for t in below:
+                nexts[t].wait_recv()
 
         @pl.when(has_next)
         def _():
-            prevs[c - 1].wait_recv()
-
-        make_pair(ext, pairs, 4 - c)
-        make_pair(ext, pairs, 6 + c)
-        add_slots(band, pairs, total, [4 - c, 4 + c])
-
-    loads[1].wait()
-    loads[2].wait()
-    for c in range(1, 5):
-        arrive(vext, vpairs, ahead, v_next, v_prev, c)
-    to_rows(total, mixed, F32)
+            for t in above:
+                prevs[t].wait_recv()
+
+    def put_mixed(p, hp, block):
+        mixed[tile_at(p), 128 * hp : 128 * hp + 128] = block
+
+    for c in (1, 2, 3):
+        arrive(v_next, v_prev, [4 - c], [c - 1])
+        make_pair(vext, vpairs, 4 - c)
+        make_pair(vext, vpairs, 6 + c)
+        add_slots(ahead, vpairs, total, [4 - c, 4 + c])
+
+    def between(h, carry):
+        extra[h] = jnp.dot(ahead[h, 0], vpairs[h, 1], preferred_element_type=F32) + jnp.dot(
+            ahead[h, 8], vpairs[h, 9], preferred_element_type=F32
+        )
+        return carry
+
+    lax.fori_loop(0, HEADS, between, 0)
+    inner_rows(total, extra, put_mixed)
+    for k in (1, 2, 4):
+        loads[k].wait()
 
     gain = gain_ref[...]
 
     def block_at(b):
         return pl.ds(pl.multiple_of(b * 128, 128), 128)
 
-    def sums(b, carry):
+    def sums(stage, b, at):
         rows = block_at(b)
         hidden = gate_ref[rows, :].astype(F32) * mixed[rows, :]
         square = hidden * hidden
         inner = gain * grad_ref[rows, :].astype(F32) * hidden
-        for k, v in ((0, square), (8, inner)):
+        for k, v in ((0, square), (4, inner)):
             half = (v[:, :128] + v[:, 128:]).T
-            chan_buf[ch, pl.ds(k + b, 1), :] = jnp.sum(half, axis=0, keepdims=True)
+            chan_buf[stage, ch, pl.ds(k + at, 1), :] = jnp.sum(half, axis=0, keepdims=True)
+
+    def inner_sums(i, carry):
+        sums(0, i + 2, i)
         return carry
 
-    lax.fori_loop(0, 8, sums, 0)
-
-    def exchange(src_of, dst, send, recv, dev_of, count):
+    def outer_sums(i, carry):
+        sums(1, i + 4 * lax.div(i, 2), i)
+        return carry
+
+    def exchange(src_of, dst, send, recv, dev_of, order):
         return [
             pltpu.make_async_remote_copy(
                 src_ref=src_of(j),
@@ -285,48 +327,63 @@
                 device_id=dev_of(j),
                 device_id_type=MESH,
             )
-            for j in range(1, count)
+            for j in order
         ]
 
-    chan_copies = exchange(
-        lambda j: chan_buf.at[ch], chan_buf.at[ch], chan_send, chan_recv, chan_dev, chans
-    )
-    for copy in chan_copies:
-        copy.start()
-    for copy in chan_copies:
-        copy.wait_recv()
-    sums_all = chan_buf[0]
-    for j in range(1, chans):
-        sums_all = sums_all + chan_buf[j]
-    scale = lax.rsqrt(sums_all[0:8] / depth + EPS)
-    row_scale[0:8, :] = scale
-    row_scale[8:16, :] = scale * scale * sums_all[8:16] / depth
+    chan_copies = [
+        exchange(
+            lambda j, k=k: chan_buf.at[k, ch],
+            chan_buf.at[k, ch],
+            chan_send.at[k],
+            chan_recv.at[k],
+            chan_dev,
+            far_first(chans),
+        )
+        for k in range(2)
+    ]
+
+    def scales(stage):
+        for copy in chan_copies[stage]:
+            copy.wait_recv()
+        sums_all = chan_buf[stage, 0]
+        for j in range(1, chans):
+            sums_all = sums_all + chan_buf[stage, j]
+        scale = lax.rsqrt(sums_all[0:4] / depth + EPS)
+        row_scale[stage, 0:4, :] = scale
+        row_scale[stage, 4:8, :] = scale * scale * sums_all[4:8] / depth
+
     gain_sum[...] = jnp.zeros((8, WIDTH), F32)
 
-    def apply(b, carry):
+    def apply(stage, b, at):
         rows = block_at(b)
 
         def column(k):
-            tall = jnp.broadcast_to(row_scale[pl.ds(k + b, 1), :], (128, 128)).T
+            tall = jnp.broadcast_to(row_scale[stage, pl.ds(k + at, 1), :], (128, 128)).T
             return jnp.concatenate([tall, tall], axis=1)
 
         scale = column(0)
-        pull = column(8)
+        pull = column(4)
         gate = gate_ref[rows, :].astype(F32)
         grad = grad_ref[rows, :].astype(F32)
         mix = mixed[rows, :]
         hidden = gate * mix
         scaled = hidden * scale
-        normed_ref[rows, :] = (scaled * gain).astype(BF16)
+        normed_out[rows, :] = (scaled * gain).astype(BF16)
         hidden_grad = scale * (gain * grad - hidden * pull)
-        gate_grad_ref[rows, :] = (hidden_grad * mix).astype(BF16)
+        gate_grad_out[rows, :] = (hidden_grad * mix).astype(BF16)
         mext[pl.ds(pl.multiple_of(ROWS + b * 128, 128), 128), :] = (hidden_grad * gate).astype(BF16)
         term = grad * scaled
         gain_sum[...] += jnp.sum(term.reshape(16, 8, WIDTH), axis=0)
-        return carry
 
     def apply_tile(t):
-        lax.fori_loop(2 * t, 2 * t + 2, apply, 0)
+        def one(i, carry):
+            if t in (1, 2):
+                apply(0, 2 * t + i, 2 * t - 2 + i)
+            else:
+                apply(1, 2 * t + i, (0 if t == 0 else 2) + i)
+            return carry
+
+        lax.fori_loop(0, 2, one, 0)
 
     def send_next(*tiles):
         @pl.when(has_next)
@@ -340,37 +397,45 @@
             for t in tiles:
                 m_prev[t].start()
 
+    lax.fori_loop(0, 4, inner_sums, 0)
+    for copy in chan_copies[0]:
+        copy.start()
+    arrive(v_next, v_prev, [0], [3])
+    make_pair(vext, vpairs, 0)
+    make_pair(vext, vpairs, 10)
+    add_slots(ahead, vpairs, total, [0, 8])
+    outer_rows(total, put_mixed)
+    lax.fori_loop(0, 4, outer_sums, 0)
+    for copy in chan_copies[1]:
+        copy.start()
+    scales(0)
+    apply_tile(1)
+    send_prev(1)
+    apply_tile(2)
+    send_next(2, 1)
+    send_prev(2)
+    scales(1)
     apply_tile(0)
     send_prev(0)
     apply_tile(3)
     send_next(3)
-    apply_tile(1)
-    send_prev(1)
-    apply_tile(2)
-    send_next(2, 1, 0)
-    send_prev(2, 3)
-    stores = [
-        pltpu.make_async_copy(normed_ref, normed_out, store_sem.at[0]),
-        pltpu.make_async_copy(gate_grad_ref, gate_grad_out, store_sem.at[1]),
-        pltpu.make_async_copy(value_grad_ref, value_grad_out, store_sem.at[2]),
-    ]
-    stores[0].start()
-    stores[1].start()
 
     for t in (4, 5, 6):
         make_pair(mext, mpairs, t)
 
     def lag_terms(h, carry):
-        lag_sum[...] = jnp.zeros((128, SPAN), F32)
         local = jnp.concatenate([mpairs[h, 4], mpairs[h, 6]], axis=1)
         for s in range(SLOTS):
             window = jnp.concatenate([vpairs[h, s], vpairs[h, s + 2]], axis=1)
             cross = lax.dot_general(
                 window, local, (((1,), (1,)), ((), ())), preferred_element_type=F32
             )
-            for k in range(2):
-                at = (17 - 2 * s - k) * 128
-                lag_sum[:, at : at + 256] += cross[128 * k : 128 * k + 128]
+            at = (17 - 2 * s) * 128
+            right = cross[0:128, 128:256]
+            lag_sum[:, at + 128 : at + 256] = right if s == 0 else right + held
+            lag_sum[:, at : at + 128] = cross[0:128, 0:128] + cross[128:256, 128:256]
+            held = cross[128:256, 0:128]
+        lag_sum[:, 0:128] = held
         eight = lag_sum[0:8, :]
         for g in range(1, 16):
             eight = eight + pltpu.roll(lag_sum[8 * g : 8 * g + 8, :], SPAN - 8 * g, 1)
@@ -394,23 +459,41 @@
         cut_src[k, cut : cut + 8, :] = gain_rows
 
     cut_copies = exchange(
-        lambda j: cut_src.at[z_of(j)], cut_buf.at[z], cut_send, cut_recv, z_dev, nz
+        lambda j: cut_src.at[z_of(j)], cut_buf.at[z], cut_send, cut_recv, z_dev, far_first(nz)
     )
     for copy in cut_copies:
         copy.start()
+    send_next(0)
+    send_prev(3)
     cut_buf[z] = cut_src[z]
 
     add_slots(behind, mpairs, total, [4], fresh=True)
+    arrive(m_next, m_prev, [2, 1, 3], [1, 2, 0])
+    for t in (1, 2, 3, 7, 8, 9):
+        make_pair(mext, mpairs, t)
+    add_slots(behind, mpairs, total, [1, 2, 3])
+    add_slots(behind, mpairs, total, [5, 6, 7])
     for copy in cut_copies:
         copy.wait_recv()
     part = cut_buf[0]
     for k in range(1, nz):
         part = part + cut_buf[k]
     all_buf[q] = part
-    all_copies = exchange(lambda j: all_buf.at[q], all_buf.at[q], all_send, all_recv, q_dev, nq)
+    all_copies = exchange(
+        lambda j: all_buf.at[q], all_buf.at[q], all_send, all_recv, q_dev, far_first_xy(nx, ny)
+    )
     for copy in all_copies:
         copy.start()
-    arrive(mext, mpairs, behind, m_next, m_prev, 1)
+    arrive(m_next, m_prev, [0], [3])
+    make_pair(mext, mpairs, 0)
+    make_pair(mext, mpairs, 10)
+    add_slots(behind, mpairs, total, [0, 8])
+
+    def put_grad(p, hp, block):
+        value_grad_out[tile_at(p), 128 * hp : 128 * hp + 128] = block.astype(BF16)
+
+    outer_rows(total, put_grad)
+    inner_rows(total, None, put_grad)
     for copy in all_copies:
         copy.wait_recv()
     part = all_buf[0]
@@ -418,16 +501,12 @@
         part = part + all_buf[k]
     gather_buf[z] = part[0:cut] * (1.0 / math.sqrt(ROWS * nseq * 64))
     gather_copies = exchange(
-        lambda j: gather_buf.at[z], gather_buf.at[z], gather_send, gather_recv, z_dev, nz
+        lambda j: gather_buf.at[z], gather_buf.at[z], gather_send, gather_recv, z_dev, far_first(nz)
     )
     for copy in gather_copies:
         copy.start()
     gains = jnp.concatenate([part[cut : cut + 1], part[cut + 1 : cut + 2]], axis=1)
     gain_grad_ref[...] = gains * (1.0 / math.sqrt(ROWS * nseq))
-    for c in (2, 3, 4):
-        arrive(mext, mpairs, behind, m_next, m_prev, c)
-    to_rows(total, value_grad_ref, BF16)
-    stores[2].start()
     for copy in gather_copies:
         copy.wait_recv()
     for row in range(64):
@@ -435,7 +514,7 @@
         k, r = divmod(row, cut)
         taps_grad_ref[h : h + 1, 128 * b : 128 * b + 128] = gather_buf[k, r : r + 1, :]
 
-    for copy in chan_copies + cut_copies + all_copies + gather_copies:
+    for copy in chan_copies[0] + chan_copies[1] + cut_copies + all_copies + gather_copies:
         copy.wait_send()
 
     @pl.when(has_next)
@@ -450,8 +529,17 @@
             v_prev[t].wait_send()
             m_prev[t].wait_send()
 
-    for store in stores:
-        store.wait()
+
+def write_out(*refs):
+    sources, targets, sem = refs[:5], refs[5:10], refs[10]
+    copies = [
+        pltpu.make_async_copy(source, target, sem.at[k])
+        for k, (source, target) in enumerate(zip(sources, targets))
+    ]
+    for copy in copies:
+        copy.start()
+    for copy in copies:
+        copy.wait()
 
 
 def on_device(dims, chans, gate_acts, value_acts, taps, norm_gain, out_grad):
@@ -459,7 +547,7 @@
     nq = ny * nx
     cut = 64 // nz
     block = jax.ShapeDtypeStruct((ROWS, WIDTH), BF16)
-    anywhere = pl.BlockSpec(memory_space=pl.ANY)
+    hbm = pl.BlockSpec(memory_space=pltpu.HBM)
     vmem = pl.BlockSpec(memory_space=pltpu.VMEM)
     dma = pltpu.SemaphoreType.DMA
     call = pl.pallas_call(
@@ -471,38 +559,37 @@
             jax.ShapeDtypeStruct((HEADS, 2048), F32),
             jax.ShapeDtypeStruct((1, WIDTH), F32),
         ),
-        in_specs=[anywhere, anywhere, vmem, vmem, anywhere],
-        out_specs=(anywhere, anywhere, anywhere, vmem, vmem),
+        in_specs=[hbm] * 5,
+        out_specs=(vmem,) * 5,
         scratch_shapes=[
             pltpu.VMEM((3 * ROWS, WIDTH), BF16),
             pltpu.VMEM((3 * ROWS, WIDTH), BF16),
             pltpu.VMEM((ROWS, WIDTH), BF16),
             pltpu.VMEM((ROWS, WIDTH), BF16),
+            pltpu.VMEM((HEADS, 2048), BF16),
+            pltpu.VMEM((1, WIDTH), F32),
             pltpu.VMEM((HEADS, SLOTS, TILE, TILE), BF16),
             pltpu.VMEM((HEADS, SLOTS, TILE, TILE), BF16),
             pltpu.VMEM((HEADS, 11, TILE, 128), BF16),
             pltpu.VMEM((HEADS, 11, TILE, 128), BF16),
             pltpu.VMEM((HEADS, TILE, TILE), F32),
+            pltpu.VMEM((HEADS, TILE, 128), F32),
             pltpu.VMEM((ROWS, WIDTH), F32),
-            pltpu.VMEM((ROWS, WIDTH), BF16),
-            pltpu.VMEM((ROWS, WIDTH), BF16),
-            pltpu.VMEM((ROWS, WIDTH), BF16),
             pltpu.VMEM((128, SPAN), F32),
-            pltpu.VMEM((chans, 16, 128), F32),
-            pltpu.VMEM((16, 128), F32),
+            pltpu.VMEM((2, chans, 8, 128), F32),
+            pltpu.VMEM((2, 8, 128), F32),
             pltpu.VMEM((8, WIDTH), F32),
             pltpu.VMEM((nz, cut + 8, 128), F32),
             pltpu.VMEM((nz, cut + 8, 128), F32),
             pltpu.VMEM((nq, cut + 8, 128), F32),
             pltpu.VMEM((nz, cut, 128), F32),
-            dma((3,)),
-            dma((3,)),
+            dma((5,)),
             dma((2, 4)),
             dma((2, 4)),
             dma((2, 4)),
             dma((2, 4)),
-            dma((chans,)),
-            dma((chans,)),
+            dma((2, chans)),
+            dma((2, chans)),
             dma((nz,)),
             dma((nz,)),
             dma((nq,)),
@@ -511,16 +598,24 @@
             dma((nz,)),
         ],
         compiler_params=pltpu.CompilerParams(
-            collective_id=0, has_side_effects=True, vmem_limit_bytes=48 * 1024 * 1024
+            collective_id=0, has_side_effects=True, vmem_limit_bytes=52 * 1024 * 1024
         ),
         cost_estimate=pl.CostEstimate(
             flops=3_700_000_000, bytes_accessed=6_000_000, transcendentals=1024
         ),
         name="toeplitz_mix",
     )
-    normed, gate_grad, value_grad, taps_grad, gain_grad = call(
-        gate_acts, value_acts, taps, norm_gain.reshape(1, WIDTH), out_grad
-    )
+    operands = (gate_acts, value_acts, taps, norm_gain.reshape(1, WIDTH), out_grad)
+    results = call(*[pltpu.with_memory_space_constraint(v, pltpu.HBM) for v in operands])
+    normed, gate_grad, value_grad, taps_grad, gain_grad = pl.pallas_call(
+        write_out,
+        out_shape=[jax.ShapeDtypeStruct(r.shape, r.dtype) for r in results],
+        in_specs=[vmem] * 5,
+        out_specs=[hbm] * 5,
+        scratch_shapes=[dma((5,))],
+        compiler_params=pltpu.CompilerParams(vmem_limit_bytes=8 * 1024 * 1024),
+        name="write_out",
+    )(*results)
     return normed, gate_grad, value_grad, taps_grad, gain_grad.reshape(WIDTH)
 
 

time: 70.6 us -> 62 us (0.88)
  the two profiles are of different devices: /device:TPU:2 before, /device:TPU:1 now
where the time goes in v2:
time: 62 us; the launch traced here: 61.9 us
  Pallas kernels  61.3 us (99%)
  between operations  0.64 us (1%)
    pallas_call x1, Pallas kernels, on_device(): call(*[pltpu.with_memory_space_constraint(v, pltpu.HBM) for v in operands])  60.1 us

profile of v2, /device:TPU:1, one launch (start us, length us, event | category | flops | bytes accessed | tf_op | source)
XLA Modules:
  0.0 61.9 jit_solution(14620787169050907406)
XLA Ops:
  0.6 60.1 %toeplitz_mix.1 = (bf16[1024,256]{1,0:T(8,128)(2,1)S(1)}, bf16[1024,256]{1,0:T(8,128)(2,1)S(1)}, bf16[1024,256]{1,0:T(8,128)(2,1)S(1)}, f32[4,2048]{1,0:T(4,128)S(1)}, f32[1,256]{1,0:T(1,128)S(1)}) custom-call(bf16[1024,256]{1,0:T(8,128)(2,1)} %gate_in.1, bf16[1024,256]{1,0:T(8,128)(2,1)} %value_in.1, bf16[4,2048]{1,0:T(4,128)(2,1)} %taps_in.1, ...), custom_call_target="tpu_custom_call" | custom-call | flops 3700000000 | bytes 6000000 | tf_op jit(solution)/shard_map/toeplitz_mix/pallas_call | solution.py:609
  60.7 1.2 %write_out.1 = (bf16[1024,256]{1,0:T(8,128)(2,1)}, bf16[1024,256]{1,0:T(8,128)(2,1)}, bf16[1024,256]{1,0:T(8,128)(2,1)}, f32[4,2048]{1,0:T(4,128)}, f32[1,256]{1,0:T(1,128)}) custom-call(bf16[1024,256]{1,0:T(8,128)(2,1)S(1)} %get-tuple-element.15.refs_0_, bf16[1024,256]{1,0:T(8,128)(2,1)S(1)} %get-tuple-element.16.refs_1_, ...), custom_call_target="tpu_custom_call" | custom-call | tf_op jit(solution)/shard_map/write_out/pallas_call | solution.py:610

commit v3 on v2

--- a/solution.py
+++ b/solution.py
@@ -181,10 +181,10 @@
 
     barrier = pltpu.get_barrier_semaphore()
     partners = (
-        [z_dev(j) for j in far_first(nz)]
+        [prev_dev, next_dev]
+        + [z_dev(j) for j in far_first(nz)]
         + [chan_dev(j) for j in far_first(chans)]
         + [q_dev(j) for j in far_first_xy(nx, ny)]
-        + [prev_dev, next_dev]
     )
     for dev in partners:
         pl.semaphore_signal(barrier, inc=1, device_id=dev, device_id_type=MESH)
@@ -416,9 +416,7 @@
     send_prev(2)
     scales(1)
     apply_tile(0)
-    send_prev(0)
     apply_tile(3)
-    send_next(3)
 
     for t in (4, 5, 6):
         make_pair(mext, mpairs, t)
@@ -463,16 +461,11 @@
     )
     for copy in cut_copies:
         copy.start()
-    send_next(0)
-    send_prev(3)
+    send_next(3, 0)
+    send_prev(0, 3)
     cut_buf[z] = cut_src[z]
 
     add_slots(behind, mpairs, total, [4], fresh=True)
-    arrive(m_next, m_prev, [2, 1, 3], [1, 2, 0])
-    for t in (1, 2, 3, 7, 8, 9):
-        make_pair(mext, mpairs, t)
-    add_slots(behind, mpairs, total, [1, 2, 3])
-    add_slots(behind, mpairs, total, [5, 6, 7])
     for copy in cut_copies:
         copy.wait_recv()
     part = cut_buf[0]
@@ -484,16 +477,11 @@
     )
     for copy in all_copies:
         copy.start()
-    arrive(m_next, m_prev, [0], [3])
-    make_pair(mext, mpairs, 0)
-    make_pair(mext, mpairs, 10)
-    add_slots(behind, mpairs, total, [0, 8])
-
-    def put_grad(p, hp, block):
-        value_grad_out[tile_at(p), 128 * hp : 128 * hp + 128] = block.astype(BF16)
-
-    outer_rows(total, put_grad)
-    inner_rows(total, None, put_grad)
+    arrive(m_next, m_prev, [2, 1, 3], [1, 2, 0])
+    for t in (1, 2, 3, 7, 8, 9):
+        make_pair(mext, mpairs, t)
+    add_slots(behind, mpairs, total, [1, 2, 3])
+    add_slots(behind, mpairs, total, [5, 6, 7])
     for copy in all_copies:
         copy.wait_recv()
     part = all_buf[0]
@@ -507,6 +495,16 @@
         copy.start()
     gains = jnp.concatenate([part[cut : cut + 1], part[cut + 1 : cut + 2]], axis=1)
     gain_grad_ref[...] = gains * (1.0 / math.sqrt(ROWS * nseq))
+    arrive(m_next, m_prev, [0], [3])
+    make_pair(mext, mpairs, 0)
+    make_pair(mext, mpairs, 10)
+    add_slots(behind, mpairs, total, [0, 8])
+
+    def put_grad(p, hp, block):
+        value_grad_out[tile_at(p), 128 * hp : 128 * hp + 128] = block.astype(BF16)
+
+    outer_rows(total, put_grad)
+    inner_rows(total, None, put_grad)
     for copy in gather_copies:
         copy.wait_recv()
     for row in range(64):

time: 62 us -> 59.5 us (0.960)
  Pallas kernels: 61.3 us -> 58.7 us
    pallas_call x1, Pallas kernels: 60.1 us -> 57.5 us  [on_device(): call(*[pltpu.with_memory_space_constraint(v, pltpu.HBM) for v in operands])]
where the time goes in v3:
time: 59.5 us; the launch traced here: 59.3 us
  Pallas kernels  58.7 us (99%)
  between operations  0.64 us (1%)
    pallas_call x1, Pallas kernels, on_device(): call(*[pltpu.with_memory_space_constraint(v, pltpu.HBM) for v in operands])  57.5 us

profile of v3, /device:TPU:1, one launch (start us, length us, event | category | flops | bytes accessed | tf_op | source)
XLA Modules:
  0.0 59.3 jit_solution(14014520854321654514)
XLA Ops:
  0.6 57.5 %toeplitz_mix.1 = (bf16[1024,256]{1,0:T(8,128)(2,1)S(1)}, bf16[1024,256]{1,0:T(8,128)(2,1)S(1)}, bf16[1024,256]{1,0:T(8,128)(2,1)S(1)}, f32[4,2048]{1,0:T(4,128)S(1)}, f32[1,256]{1,0:T(1,128)S(1)}) custom-call(bf16[1024,256]{1,0:T(8,128)(2,1)} %gate_in.1, bf16[1024,256]{1,0:T(8,128)(2,1)} %value_in.1, bf16[4,2048]{1,0:T(4,128)(2,1)} %taps_in.1, ...), custom_call_target="tpu_custom_call" | custom-call | flops 3700000000 | bytes 6000000 | tf_op jit(solution)/shard_map/toeplitz_mix/pallas_call | solution.py:607
  58.2 1.2 %write_out.1 = (bf16[1024,256]{1,0:T(8,128)(2,1)}, bf16[1024,256]{1,0:T(8,128)(2,1)}, bf16[1024,256]{1,0:T(8,128)(2,1)}, f32[4,2048]{1,0:T(4,128)}, f32[1,256]{1,0:T(1,128)}) custom-call(bf16[1024,256]{1,0:T(8,128)(2,1)S(1)} %get-tuple-element.15.refs_0_, bf16[1024,256]{1,0:T(8,128)(2,1)S(1)} %get-tuple-element.16.refs_1_, ...), custom_call_target="tpu_custom_call" | custom-call | tf_op jit(solution)/shard_map/write_out/pallas_call | solution.py:608

commit v4 on v3

--- a/solution.py
+++ b/solution.py
@@ -59,8 +59,9 @@
     for hp in range(2):
         a = ext[tile_at(t), 128 * hp : 128 * hp + 128]
         b = ext[tile_at(t + 1), 128 * hp : 128 * hp + 128]
-        pairs[2 * hp, t] = jnp.where(low, a, swap_halves(b))
-        pairs[2 * hp + 1, t] = jnp.where(low, swap_halves(a), b)
+        crossed = swap_halves(jnp.where(low, b, a))
+        pairs[2 * hp, t] = jnp.where(low, a, crossed)
+        pairs[2 * hp + 1, t] = jnp.where(low, crossed, b)
 
 
 def add_slots(band, pairs, total, slots, fresh=False):
@@ -87,19 +88,29 @@
         put(3, hp, jnp.where(low, swap_halves(a), b))
 
 
+def all_rows(total, put):
+    low = lax.broadcasted_iota(jnp.int32, (TILE, 128), 1) < 64
+    for hp in range(2):
+        for pp in range(2):
+            a = total[2 * hp, :, 128 * pp : 128 * pp + 128]
+            b = total[2 * hp + 1, :, 128 * pp : 128 * pp + 128]
+            crossed = swap_halves(jnp.where(low, b, a))
+            put(2 * pp, hp, jnp.where(low, a, crossed))
+            put(2 * pp + 1, hp, jnp.where(low, crossed, b))
+
+
 def inner_rows(total, extra, put):
     low = lax.broadcasted_iota(jnp.int32, (TILE, 128), 1) < 64
     for hp in range(2):
-        more_a = 0.0 if extra is None else extra[2 * hp]
-        more_b = 0.0 if extra is None else extra[2 * hp + 1]
-        swap_a = 0.0 if extra is None else swap_halves(more_a)
-        swap_b = 0.0 if extra is None else swap_halves(more_b)
+        more_a = extra[2 * hp]
+        more_b = extra[2 * hp + 1]
+        more = swap_halves(jnp.where(low, more_b, more_a))
         a = total[2 * hp, :, 0:128]
         b = total[2 * hp + 1, :, 0:128]
-        put(1, hp, jnp.where(low, swap_halves(a) + more_a, b + swap_b))
+        put(1, hp, jnp.where(low, swap_halves(a) + more_a, b + more))
         a = total[2 * hp, :, 128:256]
         b = total[2 * hp + 1, :, 128:256]
-        put(2, hp, jnp.where(low, a + swap_a, swap_halves(b) + more_b))
+        put(2, hp, jnp.where(low, a + more, swap_halves(b) + more_b))
 
 
 def kernel_body(
@@ -418,7 +429,7 @@
     apply_tile(0)
     apply_tile(3)
 
-    for t in (4, 5, 6):
+    for t in (4, 6):
         make_pair(mext, mpairs, t)
 
     def lag_terms(h, carry):
@@ -450,11 +461,9 @@
 
     lax.fori_loop(0, HEADS, lag_terms, 0)
     gains = jnp.sum(gain_sum[...], axis=0, keepdims=True)
-    gain_rows = jnp.concatenate(
-        [gains[:, :128], gains[:, 128:], jnp.zeros((6, 128), F32)], axis=0
-    )
+    gain_rows = jnp.concatenate([gains[:, :128], gains[:, 128:]], axis=0)
     for k in range(nz):
-        cut_src[k, cut : cut + 8, :] = gain_rows
+        cut_src[k, cut : cut + 2, :] = gain_rows
 
     cut_copies = exchange(
         lambda j: cut_src.at[z_of(j)], cut_buf.at[z], cut_send, cut_recv, z_dev, far_first(nz)
@@ -478,7 +487,7 @@
     for copy in all_copies:
         copy.start()
     arrive(m_next, m_prev, [2, 1, 3], [1, 2, 0])
-    for t in (1, 2, 3, 7, 8, 9):
+    for t in (1, 2, 3, 5, 7, 8, 9):
         make_pair(mext, mpairs, t)
     add_slots(behind, mpairs, total, [1, 2, 3])
     add_slots(behind, mpairs, total, [5, 6, 7])
@@ -503,8 +512,7 @@
     def put_grad(p, hp, block):
         value_grad_out[tile_at(p), 128 * hp : 128 * hp + 128] = block.astype(BF16)
 
-    outer_rows(total, put_grad)
-    inner_rows(total, None, put_grad)
+    all_rows(total, put_grad)
     for copy in gather_copies:
         copy.wait_recv()
     for row in range(64):
@@ -577,9 +585,9 @@
             pltpu.VMEM((2, chans, 8, 128), F32),
             pltpu.VMEM((2, 8, 128), F32),
             pltpu.VMEM((8, WIDTH), F32),
-            pltpu.VMEM((nz, cut + 8, 128), F32),
-            pltpu.VMEM((nz, cut + 8, 128), F32),
-            pltpu.VMEM((nq, cut + 8, 128), F32),
+            pltpu.VMEM((nz, cut + 2, 128), F32),
+            pltpu.VMEM((nz, cut + 2, 128), F32),
+            pltpu.VMEM((nq, cut + 2, 128), F32),
             pltpu.VMEM((nz, cut, 128), F32),
             dma((5,)),
             dma((2, 4)),

time: 59.5 us -> 58.9 us (0.990)
  Pallas kernels: 58.7 us -> 58.1 us
where the time goes in v4:
time: 58.9 us; the launch traced here: 58.8 us
  Pallas kernels  58.1 us (99%)
  between operations  0.64 us (1%)
    pallas_call x1, Pallas kernels, on_device(): call(*[pltpu.with_memory_space_constraint(v, pltpu.HBM) for v in operands])  56.9 us
    pallas_call x1, Pallas kernels, on_device(): pl.pallas_call(write_out, out_shape=[jax.ShapeDtypeStruct(r.shape, r.dtyp...  1.19 us

profile of v4, /device:TPU:1, one launch (start us, length us, event | category | flops | bytes accessed | tf_op | source)
XLA Modules:
  0.0 58.8 jit_solution(5020932652125400121)
XLA Ops:
  0.6 56.9 %toeplitz_mix.1 = (bf16[1024,256]{1,0:T(8,128)(2,1)S(1)}, bf16[1024,256]{1,0:T(8,128)(2,1)S(1)}, bf16[1024,256]{1,0:T(8,128)(2,1)S(1)}, f32[4,2048]{1,0:T(4,128)S(1)}, f32[1,256]{1,0:T(1,128)S(1)}) custom-call(bf16[1024,256]{1,0:T(8,128)(2,1)} %gate_in.1, bf16[1024,256]{1,0:T(8,128)(2,1)} %value_in.1, bf16[4,2048]{1,0:T(4,128)(2,1)} %taps_in.1, ...), custom_call_target="tpu_custom_call" | custom-call | flops 3700000000 | bytes 6000000 | tf_op jit(solution)/shard_map/toeplitz_mix/pallas_call | solution.py:615
  57.6 1.2 %write_out.1 = (bf16[1024,256]{1,0:T(8,128)(2,1)}, bf16[1024,256]{1,0:T(8,128)(2,1)}, bf16[1024,256]{1,0:T(8,128)(2,1)}, f32[4,2048]{1,0:T(4,128)}, f32[1,256]{1,0:T(1,128)}) custom-call(bf16[1024,256]{1,0:T(8,128)(2,1)S(1)} %get-tuple-element.15.refs_0_, bf16[1024,256]{1,0:T(8,128)(2,1)S(1)} %get-tuple-element.16.refs_1_, ...), custom_call_target="tpu_custom_call" | custom-call | tf_op jit(solution)/shard_map/write_out/pallas_call | solution.py:616

commit v5 on v4

--- a/solution.py
+++ b/solution.py
@@ -490,7 +490,6 @@
     for t in (1, 2, 3, 5, 7, 8, 9):
         make_pair(mext, mpairs, t)
     add_slots(behind, mpairs, total, [1, 2, 3])
-    add_slots(behind, mpairs, total, [5, 6, 7])
     for copy in all_copies:
         copy.wait_recv()
     part = all_buf[0]
@@ -504,6 +503,7 @@
         copy.start()
     gains = jnp.concatenate([part[cut : cut + 1], part[cut + 1 : cut + 2]], axis=1)
     gain_grad_ref[...] = gains * (1.0 / math.sqrt(ROWS * nseq))
+    add_slots(behind, mpairs, total, [5, 6, 7])
     arrive(m_next, m_prev, [0], [3])
     make_pair(mext, mpairs, 0)
     make_pair(mext, mpairs, 10)

time: 58.9 us -> 58.7 us (level)
  Pallas kernels: 58.1 us -> 57.5 us
    pallas_call x1, Pallas kernels: 56.9 us -> 56.3 us  [on_device(): call(*[pltpu.with_memory_space_constraint(v, pltpu.HBM) for v in operands])]
where the time goes in v5:
time: 58.7 us; the launch traced here: 58.1 us
  Pallas kernels  57.5 us (98%)
  between operations  0.64 us (1%)
    pallas_call x1, Pallas kernels, on_device(): call(*[pltpu.with_memory_space_constraint(v, pltpu.HBM) for v in operands])  56.3 us
    pallas_call x1, Pallas kernels, on_device(): pl.pallas_call(write_out, out_shape=[jax.ShapeDtypeStruct(r.shape, r.dtyp...  1.19 us

profile of v5, /device:TPU:1, one launch (start us, length us, event | category | flops | bytes accessed | tf_op | source)
XLA Modules:
  0.0 58.1 jit_solution(15447536390664654668)
XLA Ops:
  0.6 56.3 %toeplitz_mix.1 = (bf16[1024,256]{1,0:T(8,128)(2,1)S(1)}, bf16[1024,256]{1,0:T(8,128)(2,1)S(1)}, bf16[1024,256]{1,0:T(8,128)(2,1)S(1)}, f32[4,2048]{1,0:T(4,128)S(1)}, f32[1,256]{1,0:T(1,128)S(1)}) custom-call(bf16[1024,256]{1,0:T(8,128)(2,1)} %gate_in.1, bf16[1024,256]{1,0:T(8,128)(2,1)} %value_in.1, bf16[4,2048]{1,0:T(4,128)(2,1)} %taps_in.1, ...), custom_call_target="tpu_custom_call" | custom-call | flops 3700000000 | bytes 6000000 | tf_op jit(solution)/shard_map/toeplitz_mix/pallas_call | solution.py:615
  57.0 1.2 %write_out.1 = (bf16[1024,256]{1,0:T(8,128)(2,1)}, bf16[1024,256]{1,0:T(8,128)(2,1)}, bf16[1024,256]{1,0:T(8,128)(2,1)}, f32[4,2048]{1,0:T(4,128)}, f32[1,256]{1,0:T(1,128)}) custom-call(bf16[1024,256]{1,0:T(8,128)(2,1)S(1)} %get-tuple-element.15.refs_0_, bf16[1024,256]{1,0:T(8,128)(2,1)S(1)} %get-tuple-element.16.refs_1_, ...), custom_call_target="tpu_custom_call" | custom-call | tf_op jit(solution)/shard_map/write_out/pallas_call | solution.py:616
